TPU v7x, 256 devices: a whole 4x4x8 slice. The times are simulated.
256 devices in a mesh: slab: 32 (over y_hi, z, core), plane: 8 (over x, y_lo).
Axes of the slice: x: 4, y: 4 (y_hi: 2, y_lo: 2; y = y_hi * 2 + y_lo), z: 8, core: 2. Of those that a mesh axis runs over, the one named last changes fastest.
Arguments:
- features: bfloat16 [32768, 512], P(('slab', 'plane')), may hold values from -6 to 6
- gain: float32 [512], replicated, may hold values from 0.5 to 1.5
- w_query: bfloat16 [512, 512], replicated, may hold values from -0.25 to 0.25
- w_key: bfloat16 [512, 512], replicated, may hold values from -0.25 to 0.25
- w_value: bfloat16 [512, 512], replicated, may hold values from -0.25 to 0.25
- w_out: bfloat16 [512, 512], replicated, may hold values from -0.25 to 0.25
- w_face: bfloat16 [512, 512], replicated, may hold values from -0.25 to 0.25
- gamma: float32 [8], replicated, may hold values from 0.02 to 1
- positions: bfloat16 [3, 32768], P(None, ('slab', 'plane')), may hold values from 0 to 1
- key_bias: bfloat16 [8, 32768], P(None, ('slab', 'plane')), may hold values from -9 to 300
- block_mask: int32 [8, 32, 32], P('plane', 'slab'), may hold values from 0 to 1, as said below
- send_list: int32 [2, 32768], P(None, ('slab', 'plane')), may hold values from 0 to 127, as said below
- neighbour: int32 [32768], P(('slab', 'plane')), may hold values from 0 to 255, as said below
- cotangent: bfloat16 [32768, 512], P(('slab', 'plane')), may hold values from -6 to 6
Outputs:
- out: bfloat16 [32768, 512], P(('slab', 'plane'))
- d_input: bfloat16 [32768, 512], P(('slab', 'plane'))
- d_query_w: float32 [512, 512], replicated
- d_key_w: float32 [512, 512], replicated
- d_value_w: float32 [512, 512], replicated
- d_out_w: float32 [512, 512], replicated
- d_face: float32 [512, 512], replicated
Inputs may be any that keep to these rules, and one draw needn't show every extreme that they name: block_mask[p, i, j] is 0 unless slab j lies within 3 slabs of slab i around the loop; block_mask[p, i, i] = 1. `send_list`: each device's list 0 and list 1 each hold 128 distinct local atom indices. `neighbour`: ids below 128 index rows of the list received from group p - 1, the others rows of the list from group p + 1.
All inputs are finite; a program needn't handle non-finite values.
Results may differ from a plain program's by a relative error of at most 0.02.
Values may be sent and summed in bfloat16 or wider, within the bound.
No kernel may reach another device: no remote copies, remote signals or barrier semaphores. Data moves between devices by JAX's collectives and lax.ppermute only.
A program may use at most 64 MiB of HBM per device.

v0:
```python
import functools

import jax
import jax.numpy as jnp
from jax import lax
from jax.experimental import pallas as pl
from jax.experimental.pallas import tpu as pltpu
from jax.sharding import PartitionSpec as P

EPS = 1e-06
BF = jnp.bfloat16
F32 = jnp.float32
BOTH = ("slab", "plane")
N = 128
D = 512
HEADS = 8
WINDOW = 7
KEYS = WINDOW * N


def dot(a, b, ca=1, cb=0):
    return lax.dot_general(a, b, (((ca,), (cb,)), ((), ())), preferred_element_type=F32)


def pieces(value):
    high = value.astype(BF).astype(F32)
    rest = value - high
    mid = rest.astype(BF).astype(F32)
    return high, mid, rest - mid


def half_grads(stage, target, sems, start, normed_t, dk_t, dv_t, left, dq, d_mixed_b, grad_rows):
    copies = []
    rows = normed_t[pl.ds(start, 256), :]
    for number in range(5):
        if number == 0:
            grad = dot(left[0, pl.ds(start, 256), :], d_mixed_b)
        elif number == 1:
            grad = dot(left[1, pl.ds(start, 256), :], grad_rows)
        elif number == 2:
            grad = dot(rows[:, 0:N], dq)
        else:
            grad = dot(rows, (dk_t if number == 3 else dv_t)[...], 1, 1)
        grad = grad.astype(BF)
        part = slice(number * 16, (number + 1) * 16)
        for chunk in range(16):
            stage[chunk, part, :] = grad[chunk * 16 : (chunk + 1) * 16]
        copy = pltpu.make_async_copy(stage.at[:, part, :], target.at[:, part, :], sems.at[number])
        copy.start()
        copies.append(copy)
    return copies


def attend_kernel(offs_ref, allow_ref, gamma_ref, half_ref, *refs):
    pack_hbm, refs = refs[:7], refs[7:]
    cot_hbm, refs = refs[:3], refs[3:]
    list_ref, gain_ref, refs = refs[0], refs[1], refs[2:]
    weight_hbm, refs = refs[:5], refs[5:]
    send_ref, keep_ref, refs = refs[0], refs[1], refs[2:]
    out_hbm, refs = refs[:9], refs[9:]
    wk_ref, wv_ref, wq_ref, wf_ref, wo_ref = weight_refs = refs[:5]
    weight_sems, send_stage, keep_stage, send_sems, keep_sems = refs[5:10]
    normed_t_ref, dk_t_ref, dv_t_ref, dq_ref, left_ref = refs[10:15]
    normed_ref, k_ref, v_ref, augk_ref, augq_ref, ho_ref = refs[15:21]
    packs, cot_pair, cot_ref, in_sems, out_sems = refs[21:26]
    stages = refs[26:]
    sent0_ref, sent1_ref, mixed_ref, dmix_ref, dx_own_ref = stages[:5]
    dx_part_ref, dx_near1_ref, dx_near2_ref, dx_near3_ref = stages[5:]

    arrivals = []
    for number, source in enumerate(pack_hbm):
        copy = pltpu.make_async_copy(source, packs.at[number], in_sems.at[number])
        copy.start()
        arrivals.append(copy)
    loads = []
    for number, (source, target) in enumerate(zip(weight_hbm, weight_refs)):
        load = pltpu.make_async_copy(source, target, weight_sems.at[number])
        load.start()
        loads.append(load)
    cot_targets = (cot_ref, cot_pair.at[0], cot_pair.at[1])
    for number, (source, target) in enumerate(zip(cot_hbm, cot_targets)):
        load = pltpu.make_async_copy(source, target, in_sems.at[7 + number])
        load.start()
        loads.append(load)
    copies = []

    def flush(*numbers):
        for number in numbers:
            copy = pltpu.make_async_copy(stages[number], out_hbm[number], out_sems.at[number])
            copy.start()
            copies.append(copy)

    gain = gain_ref[...]
    row16 = lax.broadcasted_iota(jnp.int32, (HEADS, 16, N), 1)
    axis = jnp.where(row16 < 12, row16 // 3, 4)
    gam = jnp.concatenate([jnp.full((1, 1), gamma_ref[h], F32) for h in range(HEADS)], axis=0)
    for number in range(7):
        arrivals[number].wait()
        rows = slice(number * N, (number + 1) * N)
        x = packs[number, 0:N, :].astype(F32)
        inverse = lax.rsqrt(jnp.mean(x * x, axis=1, keepdims=True) + EPS)
        normed = (x * inverse * gain).astype(BF)
        normed_ref[rows, :] = normed
        normed_t_ref[:, rows] = normed.T
        small = packs[number, N : N + 16, 0:N].astype(F32)
        offset = offs_ref[number].astype(F32)
        px, py, pz = small[0:1], small[1:2], small[2:3]
        lifted = pz + offset
        norm2 = px * px + py * py + lifted * lifted
        bias = small[3:11] - gam * norm2
        bias = jnp.where(allow_ref[number] > 0, bias, -1e30)
        high, mid, low = pieces(bias)
        points = (px[None], py[None], pz[None])
        aug = jnp.where(axis == 3, offset, 0.0)
        for which, point in enumerate(points):
            aug = jnp.where(axis == which, point, aug)
        for which, piece in enumerate((high, mid, low)):
            aug = jnp.where(row16 == 12 + which, piece[:, None, :], aug)
        augk_ref[rows, :] = aug.reshape(N, N).T.astype(BF)
        if number == 0:
            aug = jnp.where(axis == 0, points[0], jnp.where(axis == 1, points[1], points[2]))
            high, mid, low = pieces(aug * (2.0 * gam[:, :, None]))
            aug = jnp.where(row16 % 3 == 0, high, jnp.where(row16 % 3 == 1, mid, low))
            aug = jnp.where(row16 < 12, aug, jnp.where(row16 < 15, 1.0, 0.0))
            augq_ref[...] = aug.reshape(N, N).T.astype(BF)

    for load in loads:
        load.wait()
    k_ref[...] = dot(normed_ref[...], wk_ref[...]).astype(BF)
    v_ref[...] = dot(normed_ref[...], wv_ref[...]).astype(BF)
    query = (dot(normed_ref[0:N, :], wq_ref[...]).astype(BF) * 0.125).astype(BF)

    row_n = lax.broadcasted_iota(jnp.int32, (N, N), 0)
    list0 = jnp.where(row_n == list_ref[0:1, :], 1.0, 0.0).astype(BF)
    list1 = jnp.where(row_n == list_ref[1:2, :], 1.0, 0.0).astype(BF)
    row_f = row_n.astype(F32)
    even = half_ref[1] == 0
    cot_two, cot_one = cot_pair[0], cot_pair[1]
    cot_up = jnp.where(even, cot_one, cot_two)
    cot_dn = jnp.where(even, cot_two, cot_one)
    near_up = cot_up[N : N + 16, 0:N].astype(F32)[0:1]
    near_dn = cot_dn[N : N + 16, 0:N].astype(F32)[0:1]
    pick_up = jnp.where(row_f == near_up, 1.0, 0.0).astype(BF)
    pick_dn = jnp.where(row_f + 128.0 == near_dn, 1.0, 0.0).astype(BF)
    grad_rows = dot(dot(list1, pick_up).astype(BF), cot_up[0:N, :])
    grad_rows = grad_rows + dot(dot(list0, pick_dn).astype(BF), cot_dn[0:N, :])
    grad_rows = grad_rows.astype(BF)
    d_mixed = cot_ref[...].astype(F32) + dot(grad_rows, wf_ref[...], 1, 1)
    dmix_ref[...] = d_mixed
    flush(3)
    d_mixed_b = d_mixed.astype(BF)
    d_heads = dot(d_mixed_b, wo_ref[...], 1, 1).astype(BF)

    lane = lax.broadcasted_iota(jnp.int32, (N, N), 1)
    first = lane < 64
    masks = (first, jnp.logical_not(first))
    masks_b = tuple(jnp.where(m, 1.0, 0.0).astype(BF) for m in masks)
    for pair in range(HEADS // 2):
        cols = slice(pair * N, (pair + 1) * N)
        keys = k_ref[:, cols]
        values = v_ref[:, cols]
        keys_aug = jnp.concatenate([keys, augk_ref[...]], axis=1)
        qp = query[:, cols]
        gp = d_heads[:, cols]
        q_parts = [qp * m for m in masks_b]
        g_parts = [gp * m for m in masks_b]
        probs = []
        probs_b = []
        outs = []
        for t in range(2):
            h = 2 * pair + t
            mine = jnp.where(lane // 16 == h, 1.0, 0.0).astype(BF)
            left = jnp.concatenate([q_parts[t], augq_ref[...] * mine], axis=1)
            scores = dot(left, keys_aug, 1, 1)
            top = jnp.max(scores, axis=1, keepdims=True)
            weights = jnp.exp(scores - top)
            prob = weights * (1.0 / jnp.sum(weights, axis=1, keepdims=True))
            probs.append(prob)
            probs_b.append(prob.astype(BF))
            outs.append(dot(probs_b[t], values))
        merged = jnp.where(first, outs[0], outs[1]).astype(BF)
        ho_ref[:, cols] = merged
        inner = gp.astype(F32) * merged.astype(F32)
        scores_b = []
        dqs = []
        for t in range(2):
            delta = jnp.sum(jnp.where(masks[t], inner, 0.0), axis=1, keepdims=True)
            d_prob = dot(g_parts[t], values, 1, 1)
            d_score = (probs[t] * (d_prob - delta)).astype(BF)
            scores_b.append(d_score)
            dqs.append(dot(d_score, keys))
        dq_ref[:, cols] = (jnp.where(first, dqs[0], dqs[1]) * 0.125).astype(BF)
        dk_t_ref[cols, :] = dot(
            jnp.concatenate(q_parts, axis=0), jnp.concatenate(scores_b, axis=0), 0, 0
        ).astype(BF)
        dv_t_ref[cols, :] = dot(
            jnp.concatenate(g_parts, axis=0), jnp.concatenate(probs_b, axis=0), 0, 0
        ).astype(BF)

    heads_out = ho_ref[...]
    mixed = (packs[0, 0:N, :].astype(F32) + dot(heads_out, wo_ref[...])).astype(BF)
    mixed_ref[...] = mixed
    sent0_ref[...] = dot(jnp.where(even, list1, list0), mixed, 0, 0).astype(BF)
    sent1_ref[...] = dot(jnp.where(even, list0, list1), mixed, 0, 0).astype(BF)
    flush(0, 1, 2)
    dq = dq_ref[...]
    dx_t = dot(wk_ref[...], dk_t_ref[...]) + dot(wv_ref[...], dv_t_ref[...])
    dx_own_ref[...] = dx_t[:, 0:N] + dot(wq_ref[...], dq, 1, 1)
    dx_near1_ref[...] = dx_t[:, N : 2 * N]
    dx_near2_ref[...] = dx_t[:, 2 * N : 3 * N]
    dx_near3_ref[...] = dx_t[:, 3 * N : 4 * N].astype(BF)
    for number in range(3):
        first = (4 + number) * N
        dx_part_ref[number] = dx_t[:, first : first + N].astype(BF)
    flush(4, 5, 6, 7, 8)

    left_ref[0] = heads_out.T
    left_ref[1] = mixed.T
    mine = half_ref[0]
    for stage, target, sems, side in (
        (send_stage, send_ref, send_sems, 1 - mine),
        (keep_stage, keep_ref, keep_sems, mine),
    ):
        copies += half_grads(
            stage,
            target,
            sems,
            pl.multiple_of(side * 256, 256),
            normed_t_ref,
            dk_t_ref,
            dv_t_ref,
            left_ref,
            dq,
            d_mixed_b,
            grad_rows,
        )

    for copy in copies:
        copy.wait()


def shape(dims, kind):
    return jax.ShapeDtypeStruct(dims, kind)


def whole(dims):
    return pl.BlockSpec(dims, lambda i: (0,) * len(dims), pipeline_mode=pl.Buffered(1))


def call(kernel, outs, scratch=(), smem=0, flops=1000000, limit=16, far=(), far_out=(), alias=None):
    single = not isinstance(outs, tuple)
    outs = (outs,) if single else outs

    def run(*args):
        hbm = pl.BlockSpec(memory_space=pl.ANY)
        specs = [
            pl.BlockSpec(memory_space=pltpu.SMEM) if number < smem else whole(arg.shape)
            for number, arg in enumerate(args)
        ]
        for number in far:
            specs[number] = hbm
        out_specs = [
            hbm if number in far_out else whole(out.shape) for number, out in enumerate(outs)
        ]
        results = pl.pallas_call(
            kernel,
            grid=(1,),
            out_shape=outs,
            in_specs=specs,
            out_specs=out_specs,
            input_output_aliases=alias or {},
            scratch_shapes=list(scratch),
            compiler_params=pltpu.CompilerParams(vmem_limit_bytes=limit * 1024 * 1024),
            cost_estimate=pl.CostEstimate(
                flops=flops, bytes_accessed=4000000, transcendentals=0
            ),
        )(*args)
        return results[0] if single else results

    return run


def pack_kernel(x_ref, pos_ref, bias_ref, cot_ref, near_ref, pack_ref, face_ref):
    pack_ref[0:N, :] = x_ref[...]
    face_ref[0:N, :] = cot_ref[...]
    zeros = jnp.zeros((16, D - N), BF)
    small = jnp.concatenate(
        [pos_ref[...].astype(F32), bias_ref[...].astype(F32), jnp.zeros((5, N), F32)], axis=0
    )
    pack_ref[N : N + 16, :] = jnp.concatenate([small.astype(BF), zeros], axis=1)
    near = jnp.broadcast_to(near_ref[...].astype(F32), (16, N)).astype(BF)
    face_ref[N : N + 16, :] = jnp.concatenate([near, zeros], axis=1)


def hold_kernel(keep_ref, out_ref, sem):
    copy = pltpu.make_async_copy(keep_ref, out_ref, sem)
    copy.start()
    copy.wait()


def hold(value):
    return pl.pallas_call(
        hold_kernel,
        out_shape=shape(value.shape, value.dtype),
        in_specs=[pl.BlockSpec(memory_space=pl.ANY)],
        out_specs=pl.BlockSpec(memory_space=pltpu.VMEM),
        scratch_shapes=[pltpu.SemaphoreType.DMA],
        compiler_params=pltpu.CompilerParams(vmem_limit_bytes=8 * 1024 * 1024),
        cost_estimate=pl.CostEstimate(
            flops=1000000000, bytes_accessed=4000000, transcendentals=0
        ),
    )(value)


def split_kernel(place_ref, keep_ref, recv_ref, *outs):
    for step, out in enumerate(outs):
        rows = pl.ds((place_ref[0] ^ step) * 4, 4)
        total = keep_ref[rows].astype(F32) + recv_ref[rows].astype(F32)
        out[...] = total.astype(out.dtype)


def resplit_kernel(place_ref, own_ref, a_ref, b_ref, c_ref, *outs):
    for step, out in enumerate(outs):
        chunk = place_ref[1] ^ step
        total = own_ref[chunk] + a_ref[chunk].astype(F32)
        total = total + b_ref[chunk].astype(F32) + c_ref[chunk].astype(F32)
        out[...] = total.astype(out.dtype)


def join_kernel(own_ref, a_ref, b_ref, c_ref, out_ref):
    total = own_ref[...] + a_ref[...].astype(F32)
    out_ref[...] = (total + b_ref[...].astype(F32) + c_ref[...].astype(F32)).astype(BF)


def pair_kernel(a_ref, b_ref, out_ref):
    out_ref[...] = (a_ref[...].astype(F32) + b_ref[...].astype(F32)).astype(BF)


def finish_kernel(whose, place_ref, *refs):
    parts, refs = refs[:4], refs[5 + 4 * whose :]
    outs, stage, sems = refs[:5], refs[5], refs[6]
    core = place_ref[2]
    side = core if whose == 0 else 1 - core
    copies = []
    for number in range(5):
        rows = slice(number * 16, (number + 1) * 16)
        for big in range(4):
            outer = place_ref[whose] ^ big
            for little in range(4):
                inner = place_ref[1 - whose] ^ little
                start = pl.multiple_of(outer * 64 + inner * 16, 16)
                piece = parts[big][little, rows, :]
                stage[number, pl.ds(start, 16), :] = piece.astype(F32)
        target = outs[number].at[pl.ds(pl.multiple_of(side * 256, 256), 256), :]
        copy = pltpu.make_async_copy(stage.at[number], target, sems.at[number])
        copy.start()
        copies.append(copy)
    for copy in copies:
        copy.wait()


def out_kernel(parity_ref, near_ref, one_ref, two_ref, mixed_ref, wf_ref, out_ref):
    even = parity_ref[1] == 0
    one, two = one_ref[...], two_ref[...]
    row = lax.broadcasted_iota(jnp.int32, (2 * N, N), 0)
    pick = jnp.where(row == near_ref[...], 1.0, 0.0).astype(BF)
    received = jnp.concatenate([jnp.where(even, two, one), jnp.where(even, one, two)], axis=0)
    picked = dot(pick, received, 0, 0).astype(BF)
    out_ref[...] = (mixed_ref[...].astype(F32) + dot(picked, wf_ref[...])).astype(BF)


def add_kernel(one_ref, two_ref, recv_ref, to_one_ref, to_two_ref):
    to_one_ref[...] = (one_ref[...] + recv_ref[1].astype(F32)).astype(BF)
    to_two_ref[...] = (two_ref[...] + recv_ref[2].astype(F32)).astype(BF)


def input_kernel(own_ref, *refs):
    parts, (dmix_ref, x_ref, gain_ref, out_ref) = refs[:4], refs[4:]
    total = own_ref[...]
    for part in parts:
        total = total + (part[0] if len(part.shape) == 3 else part[...]).astype(F32)
    scaled = gain_ref[...] * total.T
    x = x_ref[...].astype(F32)
    inverse = lax.rsqrt(jnp.mean(x * x, axis=1, keepdims=True) + EPS)
    drop = x * (inverse * inverse * inverse) * jnp.mean(scaled * x, axis=1, keepdims=True)
    out_ref[...] = (dmix_ref[...] + inverse * scaled - drop).astype(BF)


def device_order(slabs, planes, move):
    rings = slabs // 4
    pairs = []
    for s in range(slabs):
        for p in range(planes):
            c, z, y_hi = s % 2, (s // 2) % rings, s // (2 * rings)
            x, y_lo = p // 2, p % 2
            z2, x2, y2 = move(c, z, x, 2 * y_hi + y_lo)
            y2 = y2 % 4
            s2 = ((y2 // 2) * rings + z2 % rings) * 2 + c
            pairs.append((s * planes + p, s2 * planes + (x2 % (planes // 2)) * 2 + y2 % 2))
    return pairs


def local(
    features,
    gain,
    w_query,
    w_key,
    w_value,
    w_out,
    w_face,
    gamma,
    positions,
    key_bias,
    block_mask,
    send_list,
    neighbour,
    cotangent,
):
    slabs, planes = lax.axis_size("slab"), lax.axis_size("plane")
    slab, plane = lax.axis_index("slab"), lax.axis_index("plane")
    core = slab % 2
    rings = slabs // 4
    x_at, y_at = plane // 2, (slab // (2 * rings)) * 2 + plane % 2

    def along(value, axis, target):
        return lax.ppermute(value, axis, [(i, target(i)) for i in range(lax.axis_size(axis))])

    def partner(value):
        return along(value, "slab", lambda s: s ^ 1)

    def near1(value):
        return along(value, "slab", lambda s: (s + 1 if s % 2 else s - 1) % slabs)

    def near2(value):
        return along(value, "slab", lambda s: (s - 2 if s % 2 else s + 2) % slabs)

    def near2_back(value):
        return along(value, "slab", lambda s: (s + 2 if s % 2 else s - 2) % slabs)

    def near3(value):
        return along(value, "slab", lambda s: (s + 3 if s % 2 else s - 3) % slabs)

    def opposite3(value):
        return along(value, "slab", lambda s: (s - 3 if s % 2 else s + 3) % slabs)

    def plane_pair(value):
        return along(value, "plane", lambda p: p ^ 1)

    def plane_cross(value):
        return along(value, "plane", lambda p: (p + 1 if p % 2 else p - 1) % planes)

    def outer_step(value, k):
        pairs = device_order(
            slabs, planes, lambda c, z, x, y: (z, x, y ^ k) if c else (z, x ^ k, y)
        )
        return lax.ppermute(value, BOTH, pairs)

    def inner_step(value, k):
        pairs = device_order(
            slabs, planes, lambda c, z, x, y: (z, x ^ k, y) if c else (z, x, y ^ k)
        )
        return lax.ppermute(value, BOTH, pairs)

    def z_flip(value, k):
        pairs = device_order(slabs, planes, lambda c, z, x, y: (z ^ k, x, y))
        return lax.ppermute(value, BOTH, pairs)

    tie = lax.optimization_barrier
    packed = shape((N + 16, D), BF)
    pack, face_pack = call(pack_kernel, (packed, packed), limit=60)(
        features, positions, key_bias, cotangent, neighbour[None]
    )
    cot_one = plane_pair(face_pack)
    cot_two = plane_cross(face_pack)
    fwd2 = opposite3(pack)
    got3 = near3(pack)
    got2 = near2(pack)
    fwd1 = near2_back(pack)
    cot_one, cot_two, near_pack = tie((cot_one, cot_two, pack))
    got1 = near1(near_pack)
    fwd0 = partner(near_pack)

    offsets = (1 - 2 * core) * jnp.array([0, -1, -2, -3, 1, 2, 3], jnp.int32)
    allow = block_mask[0, 0][(slab + offsets) % slabs]
    half = jnp.stack([core, plane % 2]).astype(jnp.int32)

    weight = pltpu.VMEM((D, D), BF)
    sides = (
        shape((N, D), BF),
        shape((N, D), BF),
        shape((N, D), BF),
        shape((N, D), F32),
        shape((D, N), F32),
        shape((3, D, N), BF),
        shape((D, N), F32),
        shape((D, N), F32),
        shape((D, N), BF),
    )
    results = call(
        attend_kernel,
        (shape((16, 80, D), BF), shape((16, 80, D), BF), *sides),
        scratch=(
            *([weight] * 5),
            pltpu.SemaphoreType.DMA((5,)),
            pltpu.VMEM((16, 80, D), BF),
            pltpu.VMEM((16, 80, D), BF),
            pltpu.SemaphoreType.DMA((5,)),
            pltpu.SemaphoreType.DMA((5,)),
            pltpu.VMEM((D, KEYS), BF),
            pltpu.VMEM((D, KEYS), BF),
            pltpu.VMEM((D, KEYS), BF),
            pltpu.VMEM((N, D), BF),
            pltpu.VMEM((2, D, N), BF),
            pltpu.VMEM((KEYS, D), BF),
            pltpu.VMEM((KEYS, D), BF),
            pltpu.VMEM((KEYS, D), BF),
            pltpu.VMEM((KEYS, N), BF),
            pltpu.VMEM((N, N), BF),
            pltpu.VMEM((N, D), BF),
            pltpu.VMEM((7, N + 16, D), BF),
            pltpu.VMEM((2, N + 16, D), BF),
            pltpu.VMEM((N, D), BF),
            pltpu.SemaphoreType.DMA((10,)),
            pltpu.SemaphoreType.DMA((9,)),
            *[pltpu.VMEM(side.shape, side.dtype) for side in sides],
        ),
        smem=4,
        flops=6000000000,
        limit=60,
        far=(*range(4, 14), *range(16, 21)),
        far_out=range(11),
    )(
        offsets,
        allow,
        gamma,
        half,
        pack,
        got1,
        got2,
        got3,
        fwd0,
        fwd1,
        fwd2,
        cotangent,
        cot_two,
        cot_one,
        send_list,
        gain[None],
        w_key,
        w_value,
        w_query,
        w_face,
        w_out,
    )
    send, keep, sent0, sent1, mixed, d_mixed = results[:6]
    dx_own, dx_part, dx_near1, dx_near2, dx_near3 = results[6:]
    got = partner(send)
    keep = hold(keep)

    outer_at = jnp.where(core == 0, x_at, y_at)
    inner_at = jnp.where(core == 0, y_at, x_at)
    place = jnp.stack([outer_at, inner_at, core]).astype(jnp.int32)
    order = (2, 1, 3)
    chunk = shape((4, 80, D), BF)
    first = call(split_kernel, (shape((4, 80, D), F32), chunk, chunk, chunk), smem=1)(
        place, keep, got
    )
    first, dx_part, dx_near3 = tie((first, dx_part, dx_near3))
    got_first = [outer_step(first[k], k) for k in order]
    back = partner(dx_part)
    back3 = near3(dx_near3)
    got_first, back, back3 = tie((got_first, back, back3))

    chunk = shape((80, D), BF)
    second = call(resplit_kernel, (shape((80, D), F32), chunk, chunk, chunk), smem=1)(
        place, first[0], *got_first
    )
    second, sent0, sent1 = tie((second, sent0, sent1))
    got_second = [inner_step(second[k], k) for k in order]
    face_one = plane_pair(sent0)
    face_two = plane_cross(sent1)
    got_second, face_one, face_two = tie((got_second, face_one, face_two))
    total = call(join_kernel, chunk)(second[0], *got_second)
    total = call(pair_kernel, chunk)(total, z_flip(total, 1))
    total, face_one, face_two = tie((total, face_one, face_two))
    near = z_flip(total, 2)
    out = call(out_kernel, shape((N, D), BF), smem=1)(
        half, neighbour[None], face_one, face_two, mixed, w_face
    )
    near, out = tie((near, out))
    total = call(pair_kernel, chunk)(total, near)
    total, dx_near1, dx_near2 = tie((total, dx_near1, dx_near2))
    near = z_flip(total, 4)
    to_one, to_two = call(add_kernel, (shape((D, N), BF),) * 2)(dx_near1, dx_near2, back)
    near, to_one, to_two = tie((near, to_one, to_two))
    total = call(pair_kernel, chunk)(total, near)

    total, meet = tie((total, partner(total)))
    inner = {0: total}
    for k in order:
        inner[k] = inner_step(total, k)
    block = jnp.stack([inner[k] for k in range(4)])
    block, to_one, to_two = tie((block, to_one, to_two))
    outer = {0: block}
    for k in order:
        outer[k] = outer_step(block, k)
    back1 = near1(to_one)
    back2 = near2_back(to_two)
    mine = [outer[k] for k in range(4)]
    d_input = call(input_kernel, shape((N, D), BF))(
        dx_own, back, back1, back2, back3, d_mixed, features, gain[None]
    )
    mine, d_input = tie((mine, d_input))
    other = partner(mine)
    grads = (shape((D, D), F32),) * 5
    scratch = (pltpu.VMEM((5, 256, D), F32), pltpu.SemaphoreType.DMA((5,)))
    every = tuple(range(5))
    grads = call(
        functools.partial(finish_kernel, 0), grads, scratch, smem=1, far=(5,), far_out=every
    )(place, *mine, meet)
    weights = call(
        functools.partial(finish_kernel, 1),
        (shape((D, D), F32),) * 5,
        scratch,
        smem=1,
        far=tuple(range(5, 10)),
        far_out=every,
        alias={5 + number: number for number in every},
    )(place, *other, *grads)
    d_out_w, d_face, d_query_w, d_key_w, d_value_w = weights

    return (out, d_input, d_query_w, d_key_w, d_value_w, d_out_w, d_face)


def solution(mesh):
    rows = P(BOTH, None)
    return jax.shard_map(
        local,
        mesh=mesh,
        in_specs=(
            rows,
            P(),
            P(),
            P(),
            P(),
            P(),
            P(),
            P(),
            P(None, BOTH),
            P(None, BOTH),
            P("plane", "slab", None),
            P(None, BOTH),
            P(BOTH),
            rows,
        ),
        out_specs=(rows, rows, P(), P(), P(), P(), P()),
        check_vma=False,
    )
```

profile of v0, /device:TPU:1, one launch (start us, length us, event | category | flops | bytes accessed | tf_op | source)
XLA Modules:
  0.0 126.8 jit_solution(5084934520187065949)
XLA Ops:
  0.6 1.7 %shard_map.198 = (bf16[144,512]{1,0:T(8,128)(2,1)}, bf16[144,512]{1,0:T(8,128)(2,1)}) custom-call(bf16[128,512]{1,0:T(8,128)(2,1)} %refs_5_.1, bf16[3,128]{1,0:T(4,128)(2,1)} %pos_ref.1, bf16[8,128]{1,0:T(8,128)(2,1)} %bias_ref.1, bf16[128,512]{1,0:T(8,128)(2,1)} %refs_7_.1, s32[1,128]{1,0:T(1,128)} %bitcast.13), custom_call_target="tpu_custom_call" | custom-call | flops 1000000 | bytes 4000000 | tf_op jit(solution)/shard_map/pallas_call | solution.py:265
  2.4 4.3 %collective-permute-start.1 = (bf16[144,512]{1,0:T(8,128)(2,1)}, bf16[144,512]{1,0:T(8,128)(2,1)S(1)}, u32[]{:S(2)}, u32[]{:S(2)}) collective-permute-start(bf16[144,512]{1,0:T(8,128)(2,1)} %get-tuple-element.87), channel_id=1, source_target_pairs={{0,7},{1,2},{2,1},{3,4},{4,3},{5,6},{6,5},{7,0},{8,15},{9,10},{10,... | collective-permute-start | bytes 442376 | tf_op jit(solution)/shard_map/ppermute | solution.py:426
  6.7 8.8 %collective-permute-start.7 = (bf16[144,512]{1,0:T(8,128)(2,1)}, bf16[144,512]{1,0:T(8,128)(2,1)S(1)}, u32[]{:S(2)}, u32[]{:S(2)}) collective-permute-start(bf16[144,512]{1,0:T(8,128)(2,1)} %get-tuple-element.88.refs_0_), channel_id=1, source_target_pairs={{0,24},{8,240},{16,40},{24,0},{32,56},{40,16},{48,72},{56,32},{64,... | collective-permute-start | bytes 442376 | tf_op jit(solution)/shard_map/ppermute | solution.py:426
  16.7 5.1 %collective-permute-start.3 = (bf16[144,512]{1,0:T(8,128)(2,1)}, bf16[144,512]{1,0:T(8,128)(2,1)S(1)}, u32[]{:S(2)}, u32[]{:S(2)}) collective-permute-start(bf16[144,512]{1,0:T(8,128)(2,1)} %get-tuple-element.88.refs_0_), channel_id=1, source_target_pairs={{0,16},{8,248},{16,32},{24,8},{32,48},{40,24},{48,64},{56,40},{64,... | collective-permute-start | bytes 442376 | tf_op jit(solution)/shard_map/ppermute | solution.py:426
  21.8 1.9 %collective-permute-start.5 = (bf16[144,512]{1,0:T(8,128)(2,1)}, bf16[144,512]{1,0:T(8,128)(2,1)S(1)}, u32[]{:S(2)}, u32[]{:S(2)}) collective-permute-start(bf16[144,512]{1,0:T(8,128)(2,1)} %get-tuple-element.88.refs_0_), channel_id=1, source_target_pairs={{0,8},{8,0},{16,24},{24,16},{32,40},{40,32},{48,56},{56,48},{64,72... | collective-permute-start | bytes 442376 | tf_op jit(solution)/shard_map/ppermute | solution.py:426
  25.8 2.7 %collective-permute-done.2.refs_1_ = bf16[144,512]{1,0:T(8,128)(2,1)S(1)} collective-permute-done((bf16[144,512]{1,0:T(8,128)(2,1)}, bf16[144,512]{1,0:T(8,128)(2,1)S(1)}, u32[]{:S(2)}, u32[]{:S(2)}) %collective-permute-start.2) | collective-permute-done | bytes 147488 | tf_op jit(solution)/shard_map/ppermute | solution.py:426
  29.1 16.1 %shard_map.199 = (bf16[16,80,512]{2,1,0:T(8,128)(2,1)}, bf16[16,80,512]{2,1,0:T(8,128)(2,1)}, bf16[128,512]{1,0:T(8,128)(2,1)}, bf16[128,512]{1,0:T(8,128)(2,1)}...) custom-call(s32[7]{0:T(128)} %get-tuple-element.166.offs_ref, ...), custom_call_target="tpu_custom_call" | custom-call | flops 6000000000 | bytes 4000000 | tf_op jit(solution)/shard_map/pallas_call | solution.py:265
  45.2 4.0 %collective-permute-start.8 = (bf16[16,80,512]{2,1,0:T(8,128)(2,1)}, bf16[16,80,512]{2,1,0:T(8,128)(2,1)S(1)}, u32[]{:S(2)}, u32[]{:S(2)}) collective-permute-start(bf16[16,80,512]{2,1,0:T(8,128)(2,1)} %get-tuple-element.92), channel_id=1, source_target_pairs={{0,8},{8,0},{16,24},{24,16},{32,40},{40,32},{48,56},{56,48},{64,72... | collective-permute-start | bytes 3932168 | tf_op jit(solution)/shard_map/ppermute | solution.py:426
  53.9 1.7 %collective-permute-start.10 = (bf16[4,80,512]{2,1,0:T(8,128)(2,1)S(1)}, bf16[4,80,512]{2,1,0:T(8,128)(2,1)S(1)}, u32[]{:S(2)}, u32[]{:S(2)}) collective-permute-start(bf16[4,80,512]{2,1,0:T(8,128)(2,1)S(1)} %get-tuple-element.101), channel_id=1, source_target_pairs={{0,2},{1,3},{2,0},{3,1},{4,6},{5,7},{6,4},{7,5},{8,9},{9,8},{10,11... | collective-permute-start | bytes 983048 | tf_op jit(solution)/shard_map/ppermute | solution.py:456
  57.1 6.0 %collective-permute-done.13.refs_3_ = bf16[512,128]{1,0:T(8,128)(2,1)S(1)} collective-permute-done((bf16[512,128]{1,0:T(8,128)(2,1)S(1)}, bf16[512,128]{1,0:T(8,128)(2,1)S(1)}, u32[]{:S(2)}, u32[]{:S(2)}) %collective-permute-start.13) | collective-permute-done | bytes 131104 | tf_op jit(solution)/shard_map/ppermute | solution.py:426
  74.5 3.3 %collective-permute-done.19.b_ref = bf16[80,512]{1,0:T(8,128)(2,1)S(1)} collective-permute-done((bf16[80,512]{1,0:T(8,128)(2,1)S(1)}, bf16[80,512]{1,0:T(8,128)(2,1)S(1)}, u32[]{:S(2)}, u32[]{:S(2)}) %collective-permute-start.19) | collective-permute-done | bytes 81952 | tf_op jit(solution)/shard_map/ppermute | solution.py:466
  78.0 1.6 %shard_map.205 = bf16[128,512]{1,0:T(8,128)(2,1)} custom-call(s32[2]{0:T(128)S(1)} %copy-done.10, s32[1,128]{1,0:T(1,128)S(1)} %bitcast.14, bf16[128,512]{1,0:T(8,128)(2,1)S(1)} %collective-permute-done.17.one_ref, bf16[128,512]{1,0:T(8,128)(2,1)S(1)} %collective-permute-done.18.two_ref, bf16[128,512]{1,0:T(8,128)(2,1)S(1)} %copy-done.7, ...), custom_call_target="tpu_custom_call" | custom-call | flops 1000000 | bytes 4000000 | tf_op jit(solution)/shard_map/pallas_call | solution.py:265
  79.6 3.1 %collective-permute-done.20.b_ref = bf16[80,512]{1,0:T(8,128)(2,1)S(1)} collective-permute-done((bf16[80,512]{1,0:T(8,128)(2,1)S(1)}, bf16[80,512]{1,0:T(8,128)(2,1)S(1)}, u32[]{:S(2)}, u32[]{:S(2)}) %collective-permute-start.20) | collective-permute-done | bytes 81952 | tf_op jit(solution)/shard_map/ppermute | solution.py:466
  83.1 7.3 %collective-permute-done.21.b_ref = bf16[80,512]{1,0:T(8,128)(2,1)S(1)} collective-permute-done((bf16[80,512]{1,0:T(8,128)(2,1)S(1)}, bf16[80,512]{1,0:T(8,128)(2,1)S(1)}, u32[]{:S(2)}, u32[]{:S(2)}) %collective-permute-start.21) | collective-permute-done | bytes 81952 | tf_op jit(solution)/shard_map/ppermute | solution.py:466
  90.5 7.6 %collective-permute-start.22 = (bf16[80,512]{1,0:T(8,128)(2,1)S(1)}, bf16[80,512]{1,0:T(8,128)(2,1)S(1)}, u32[]{:S(2)}, u32[]{:S(2)}) collective-permute-start(bf16[80,512]{1,0:T(8,128)(2,1)S(1)} %shard_map.208), channel_id=1, source_target_pairs={{0,8},{8,0},{16,24},{24,16},{32,40},{40,32},{48,56},{56,48},{64,72... | collective-permute-start | bytes 245768 | tf_op jit(solution)/shard_map/ppermute | solution.py:426
  99.0 1.6 %collective-permute-start.25 = (bf16[80,512]{1,0:T(8,128)(2,1)S(1)}, bf16[80,512]{1,0:T(8,128)(2,1)S(1)}, u32[]{:S(2)}, u32[]{:S(2)}) collective-permute-start(bf16[80,512]{1,0:T(8,128)(2,1)S(1)} %shard_map.208), channel_id=1, source_target_pairs={{0,129},{1,128},{2,131},{3,130},{4,133},{5,132},{6,135},{7,134},{8... | collective-permute-start | bytes 245768 | tf_op jit(solution)/shard_map/ppermute | solution.py:462
  102.3 1.5 %collective-permute-done.25 = bf16[80,512]{1,0:T(8,128)(2,1)S(1)} collective-permute-done((bf16[80,512]{1,0:T(8,128)(2,1)S(1)}, bf16[80,512]{1,0:T(8,128)(2,1)S(1)}, u32[]{:S(2)}, u32[]{:S(2)}) %collective-permute-start.25) | collective-permute-done | bytes 81952 | tf_op jit(solution)/shard_map/ppermute | solution.py:462
  103.8 1.6 %collective-permute-done.24 = bf16[80,512]{1,0:T(8,128)(2,1)S(1)} collective-permute-done((bf16[80,512]{1,0:T(8,128)(2,1)S(1)}, bf16[80,512]{1,0:T(8,128)(2,1)S(1)}, u32[]{:S(2)}, u32[]{:S(2)}) %collective-permute-start.24) | collective-permute-done | bytes 81952 | tf_op jit(solution)/shard_map/ppermute | solution.py:462
  105.4 3.1 %collective-permute-start.28 = (bf16[4,80,512]{2,1,0:T(8,128)(2,1)S(1)}, bf16[4,80,512]{2,1,0:T(8,128)(2,1)S(1)}, u32[]{:S(2)}, u32[]{:S(2)}) collective-permute-start(bf16[4,80,512]{2,1,0:T(8,128)(2,1)S(1)} %pad_maximum_fusion.refs_0_), channel_id=1, source_target_pairs={{0,6},{1,7},{2,4},{3,5},{4,2},{5,3},{6,0},{7,1},{8,137},{9,136},{1... | collective-permute-start | bytes 983048 | tf_op jit(solution)/shard_map/ppermute | solution.py:456
  109.2 2.8 %collective-permute-start.29 = (bf16[512,128]{1,0:T(8,128)(2,1)S(1)}, bf16[512,128]{1,0:T(8,128)(2,1)S(1)}, u32[]{:S(2)}, u32[]{:S(2)}) collective-permute-start(bf16[512,128]{1,0:T(8,128)(2,1)S(1)} %get-tuple-element.145), channel_id=1, source_target_pairs={{0,248},{8,16},{16,8},{24,32},{32,24},{40,48},{48,40},{56,64},{64,... | collective-permute-start | bytes 393224 | tf_op jit(solution)/shard_map/ppermute | solution.py:426
  111.9 2.9 %collective-permute-done.29.refs_1_ = bf16[512,128]{1,0:T(8,128)(2,1)S(1)} collective-permute-done((bf16[512,128]{1,0:T(8,128)(2,1)S(1)}, bf16[512,128]{1,0:T(8,128)(2,1)S(1)}, u32[]{:S(2)}, u32[]{:S(2)}) %collective-permute-start.29) | collective-permute-done | bytes 131104 | tf_op jit(solution)/shard_map/ppermute | solution.py:426
  114.9 5.5 %collective-permute-done.30.refs_2_ = bf16[512,128]{1,0:T(8,128)(2,1)S(1)} collective-permute-done((bf16[512,128]{1,0:T(8,128)(2,1)S(1)}, bf16[512,128]{1,0:T(8,128)(2,1)S(1)}, u32[]{:S(2)}, u32[]{:S(2)}) %collective-permute-start.30) | collective-permute-done | bytes 131104 | tf_op jit(solution)/shard_map/ppermute | solution.py:426
  122.4 2.1 %shard_map.210 = (f32[512,512]{1,0:T(8,128)}, f32[512,512]{1,0:T(8,128)}, f32[512,512]{1,0:T(8,128)}, f32[512,512]{1,0:T(8,128)}, f32[512,512]{1,0:T(8,128)}) custom-call(s32[3]{0:T(128)S(1)} %pad_add_fusion.place_ref, bf16[4,80,512]{2,1,0:T(8,128)(2,1)S(1)} %pad_maximum_fusion.refs_0_, bf16[4,80,512]{2,1,0:T(8,128)(2,1)S(1)} %collective-permute-done.26.refs_1_, ...), custom_call_target="tpu_custom_call" | custom-call | flops 1000000 | bytes 4000000 | tf_op jit(solution)/shard_map/pallas_call | solution.py:265
  124.5 2.1 %shard_map.211 = (f32[512,512]{1,0:T(8,128)}, f32[512,512]{1,0:T(8,128)}, f32[512,512]{1,0:T(8,128)}, f32[512,512]{1,0:T(8,128)}, f32[512,512]{1,0:T(8,128)}) custom-call(s32[3]{0:T(128)S(1)} %pad_add_fusion.place_ref, ...), custom_call_target="tpu_custom_call", output_to_operand_aliasing={{0}: (5, {}), {1}: (6, {}), {2}: (7, {}), {3}: (8, {}), {4}... | custom-call | flops 1000000 | bytes 4000000 | tf_op jit(solution)/shard_map/pallas_call | solution.py:265
  (114 shorter events, 27.3 us)
Async XLA Ops:
  2.4 14.3 %collective-permute-start.1 = (bf16[144,512]{1,0:T(8,128)(2,1)}, bf16[144,512]{1,0:T(8,128)(2,1)S(1)}, u32[]{:S(2)}, u32[]{:S(2)}) collective-permute-start(bf16[144,512]{1,0:T(8,128)(2,1)} %get-tuple-element.87), channel_id=1, source_target_pairs={{0,7},{1,2},{2,1},{3,4},{4,3},{5,6},{6,5},{7,0},{8,15},{9,10},{10,... | collective-permute-start | bytes 442376 | tf_op jit(solution)/shard_map/ppermute | solution.py:426
  6.7 15.1 %collective-permute-start = (bf16[144,512]{1,0:T(8,128)(2,1)}, bf16[144,512]{1,0:T(8,128)(2,1)S(1)}, u32[]{:S(2)}, u32[]{:S(2)}) collective-permute-start(bf16[144,512]{1,0:T(8,128)(2,1)} %get-tuple-element.87), channel_id=1, source_target_pairs={{0,1},{1,0},{2,3},{3,2},{4,5},{5,4},{6,7},{7,6},{8,9},{9,8},{10,11... | collective-permute-start | bytes 442376 | tf_op jit(solution)/shard_map/ppermute | solution.py:426
  6.7 17.0 %collective-permute-start.7 = (bf16[144,512]{1,0:T(8,128)(2,1)}, bf16[144,512]{1,0:T(8,128)(2,1)S(1)}, u32[]{:S(2)}, u32[]{:S(2)}) collective-permute-start(bf16[144,512]{1,0:T(8,128)(2,1)} %get-tuple-element.88.refs_0_), channel_id=1, source_target_pairs={{0,24},{8,240},{16,40},{24,0},{32,56},{40,16},{48,72},{56,32},{64,... | collective-permute-start | bytes 442376 | tf_op jit(solution)/shard_map/ppermute | solution.py:426
  15.5 10.0 %collective-permute-start.6 = (bf16[144,512]{1,0:T(8,128)(2,1)}, bf16[144,512]{1,0:T(8,128)(2,1)S(1)}, u32[]{:S(2)}, u32[]{:S(2)}) collective-permute-start(bf16[144,512]{1,0:T(8,128)(2,1)} %get-tuple-element.88.refs_0_), channel_id=1, source_target_pairs={{0,240},{8,24},{16,0},{24,40},{32,16},{40,56},{48,32},{56,72},{64,... | collective-permute-start | bytes 442376 | tf_op jit(solution)/shard_map/ppermute | solution.py:426
  15.5 10.0 %collective-permute-start.4 = (bf16[144,512]{1,0:T(8,128)(2,1)}, bf16[144,512]{1,0:T(8,128)(2,1)S(1)}, u32[]{:S(2)}, u32[]{:S(2)}) collective-permute-start(bf16[144,512]{1,0:T(8,128)(2,1)} %get-tuple-element.88.refs_0_), channel_id=1, source_target_pairs={{0,232},{8,32},{16,248},{24,48},{32,8},{40,64},{48,24},{56,80},{64... | collective-permute-start | bytes 442376 | tf_op jit(solution)/shard_map/ppermute | solution.py:426
  16.7 9.1 %collective-permute-start.3 = (bf16[144,512]{1,0:T(8,128)(2,1)}, bf16[144,512]{1,0:T(8,128)(2,1)S(1)}, u32[]{:S(2)}, u32[]{:S(2)}) collective-permute-start(bf16[144,512]{1,0:T(8,128)(2,1)} %get-tuple-element.88.refs_0_), channel_id=1, source_target_pairs={{0,16},{8,248},{16,32},{24,8},{32,48},{40,24},{48,64},{56,40},{64,... | collective-permute-start | bytes 442376 | tf_op jit(solution)/shard_map/ppermute | solution.py:426
  45.2 6.9 %collective-permute-start.8 = (bf16[16,80,512]{2,1,0:T(8,128)(2,1)}, bf16[16,80,512]{2,1,0:T(8,128)(2,1)S(1)}, u32[]{:S(2)}, u32[]{:S(2)}) collective-permute-start(bf16[16,80,512]{2,1,0:T(8,128)(2,1)} %get-tuple-element.92), channel_id=1, source_target_pairs={{0,8},{8,0},{16,24},{24,16},{32,40},{40,32},{48,56},{56,48},{64,72... | collective-permute-start | bytes 3932168 | tf_op jit(solution)/shard_map/ppermute | solution.py:426
  53.1 11.7 %collective-permute-start.12 = (bf16[3,512,128]{2,1,0:T(8,128)(2,1)S(1)}, bf16[3,512,128]{2,1,0:T(8,128)(2,1)S(1)}, u32[]{:S(2)}, u32[]{:S(2)}) collective-permute-start(bf16[3,512,128]{2,1,0:T(8,128)(2,1)S(1)} %copy-done.12), channel_id=1, source_target_pairs={{0,8},{8,0},{16,24},{24,16},{32,40},{40,32},{48,56},{56,48},{64,72... | collective-permute-start | bytes 1179656 | tf_op jit(solution)/shard_map/ppermute | solution.py:426
  53.5 9.6 %collective-permute-start.9 = (bf16[4,80,512]{2,1,0:T(8,128)(2,1)S(1)}, bf16[4,80,512]{2,1,0:T(8,128)(2,1)S(1)}, u32[]{:S(2)}, u32[]{:S(2)}) collective-permute-start(bf16[4,80,512]{2,1,0:T(8,128)(2,1)S(1)} %get-tuple-element.100), channel_id=1, source_target_pairs={{0,4},{1,5},{2,6},{3,7},{4,0},{5,1},{6,2},{7,3},{8,136},{9,137},{1... | collective-permute-start | bytes 983048 | tf_op jit(solution)/shard_map/ppermute | solution.py:456
  53.9 10.0 %collective-permute-start.10 = (bf16[4,80,512]{2,1,0:T(8,128)(2,1)S(1)}, bf16[4,80,512]{2,1,0:T(8,128)(2,1)S(1)}, u32[]{:S(2)}, u32[]{:S(2)}) collective-permute-start(bf16[4,80,512]{2,1,0:T(8,128)(2,1)S(1)} %get-tuple-element.101), channel_id=1, source_target_pairs={{0,2},{1,3},{2,0},{3,1},{4,6},{5,7},{6,4},{7,5},{8,9},{9,8},{10,11... | collective-permute-start | bytes 983048 | tf_op jit(solution)/shard_map/ppermute | solution.py:456
  55.6 9.1 %collective-permute-start.11 = (bf16[4,80,512]{2,1,0:T(8,128)(2,1)S(1)}, bf16[4,80,512]{2,1,0:T(8,128)(2,1)S(1)}, u32[]{:S(2)}, u32[]{:S(2)}) collective-permute-start(bf16[4,80,512]{2,1,0:T(8,128)(2,1)S(1)} %get-tuple-element.102), channel_id=1, source_target_pairs={{0,6},{1,7},{2,4},{3,5},{4,2},{5,3},{6,0},{7,1},{8,137},{9,136},{1... | collective-permute-start | bytes 983048 | tf_op jit(solution)/shard_map/ppermute | solution.py:456
  57.1 6.0 %collective-permute-start.13 = (bf16[512,128]{1,0:T(8,128)(2,1)S(1)}, bf16[512,128]{1,0:T(8,128)(2,1)S(1)}, u32[]{:S(2)}, u32[]{:S(2)}) collective-permute-start(bf16[512,128]{1,0:T(8,128)(2,1)S(1)} %copy-done.23), channel_id=1, source_target_pairs={{0,232},{8,32},{16,248},{24,48},{32,8},{40,64},{48,24},{56,80},{64... | collective-permute-start | bytes 393224 | tf_op jit(solution)/shard_map/ppermute | solution.py:426
  65.5 8.9 %collective-permute-start.17 = (bf16[128,512]{1,0:T(8,128)(2,1)S(1)}, bf16[128,512]{1,0:T(8,128)(2,1)S(1)}, u32[]{:S(2)}, u32[]{:S(2)}) collective-permute-start(bf16[128,512]{1,0:T(8,128)(2,1)S(1)} %copy-done.22), channel_id=1, source_target_pairs={{0,1},{1,0},{2,3},{3,2},{4,5},{5,4},{6,7},{7,6},{8,9},{9,8},{10,11... | collective-permute-start | bytes 393224 | tf_op jit(solution)/shard_map/ppermute | solution.py:426
  66.7 7.6 %collective-permute-start.18 = (bf16[128,512]{1,0:T(8,128)(2,1)S(1)}, bf16[128,512]{1,0:T(8,128)(2,1)S(1)}, u32[]{:S(2)}, u32[]{:S(2)}) collective-permute-start(bf16[128,512]{1,0:T(8,128)(2,1)S(1)} %copy-done.21), channel_id=1, source_target_pairs={{0,7},{1,2},{2,1},{3,4},{4,3},{5,6},{6,5},{7,0},{8,15},{9,10},{10,... | collective-permute-start | bytes 393224 | tf_op jit(solution)/shard_map/ppermute | solution.py:426
  69.5 4.8 %collective-permute-start.16 = (bf16[80,512]{1,0:T(8,128)(2,1)S(1)}, bf16[80,512]{1,0:T(8,128)(2,1)S(1)}, u32[]{:S(2)}, u32[]{:S(2)}) collective-permute-start(bf16[80,512]{1,0:T(8,128)(2,1)S(1)} %get-tuple-element.117), channel_id=1, source_target_pairs={{0,129},{1,128},{2,131},{3,130},{4,133},{5,132},{6,135},{7,134},{8... | collective-permute-start | bytes 245768 | tf_op jit(solution)/shard_map/ppermute | solution.py:462
  77.8 4.9 %collective-permute-start.20 = (bf16[80,512]{1,0:T(8,128)(2,1)S(1)}, bf16[80,512]{1,0:T(8,128)(2,1)S(1)}, u32[]{:S(2)}, u32[]{:S(2)}) collective-permute-start(bf16[80,512]{1,0:T(8,128)(2,1)S(1)} %shard_map.204.a_ref), channel_id=1, source_target_pairs={{0,32},{1,33},{2,34},{3,35},{4,36},{5,37},{6,38},{7,39},{8,40},{9,... | collective-permute-start | bytes 245768 | tf_op jit(solution)/shard_map/ppermute | solution.py:466
  82.7 7.7 %collective-permute-start.21 = (bf16[80,512]{1,0:T(8,128)(2,1)S(1)}, bf16[80,512]{1,0:T(8,128)(2,1)S(1)}, u32[]{:S(2)}, u32[]{:S(2)}) collective-permute-start(bf16[80,512]{1,0:T(8,128)(2,1)S(1)} %shard_map.206.a_ref), channel_id=1, source_target_pairs={{0,64},{1,65},{2,66},{3,67},{4,68},{5,69},{6,70},{7,71},{8,72},{9,... | collective-permute-start | bytes 245768 | tf_op jit(solution)/shard_map/ppermute | solution.py:466
  90.5 8.5 %collective-permute-start.22 = (bf16[80,512]{1,0:T(8,128)(2,1)S(1)}, bf16[80,512]{1,0:T(8,128)(2,1)S(1)}, u32[]{:S(2)}, u32[]{:S(2)}) collective-permute-start(bf16[80,512]{1,0:T(8,128)(2,1)S(1)} %shard_map.208), channel_id=1, source_target_pairs={{0,8},{8,0},{16,24},{24,16},{32,40},{40,32},{48,56},{56,48},{64,72... | collective-permute-start | bytes 245768 | tf_op jit(solution)/shard_map/ppermute | solution.py:426
  99.0 4.8 %collective-permute-start.25 = (bf16[80,512]{1,0:T(8,128)(2,1)S(1)}, bf16[80,512]{1,0:T(8,128)(2,1)S(1)}, u32[]{:S(2)}, u32[]{:S(2)}) collective-permute-start(bf16[80,512]{1,0:T(8,128)(2,1)S(1)} %shard_map.208), channel_id=1, source_target_pairs={{0,129},{1,128},{2,131},{3,130},{4,133},{5,132},{6,135},{7,134},{8... | collective-permute-start | bytes 245768 | tf_op jit(solution)/shard_map/ppermute | solution.py:462
  105.4 15.8 %collective-permute-start.28 = (bf16[4,80,512]{2,1,0:T(8,128)(2,1)S(1)}, bf16[4,80,512]{2,1,0:T(8,128)(2,1)S(1)}, u32[]{:S(2)}, u32[]{:S(2)}) collective-permute-start(bf16[4,80,512]{2,1,0:T(8,128)(2,1)S(1)} %pad_maximum_fusion.refs_0_), channel_id=1, source_target_pairs={{0,6},{1,7},{2,4},{3,5},{4,2},{5,3},{6,0},{7,1},{8,137},{9,136},{1... | collective-permute-start | bytes 983048 | tf_op jit(solution)/shard_map/ppermute | solution.py:456
  108.5 12.8 %collective-permute-start.27 = (bf16[4,80,512]{2,1,0:T(8,128)(2,1)S(1)}, bf16[4,80,512]{2,1,0:T(8,128)(2,1)S(1)}, u32[]{:S(2)}, u32[]{:S(2)}) collective-permute-start(bf16[4,80,512]{2,1,0:T(8,128)(2,1)S(1)} %pad_maximum_fusion.refs_0_), channel_id=1, source_target_pairs={{0,4},{1,5},{2,6},{3,7},{4,0},{5,1},{6,2},{7,3},{8,136},{9,137},{1... | collective-permute-start | bytes 983048 | tf_op jit(solution)/shard_map/ppermute | solution.py:456
  108.5 12.8 %collective-permute-start.26 = (bf16[4,80,512]{2,1,0:T(8,128)(2,1)S(1)}, bf16[4,80,512]{2,1,0:T(8,128)(2,1)S(1)}, u32[]{:S(2)}, u32[]{:S(2)}) collective-permute-start(bf16[4,80,512]{2,1,0:T(8,128)(2,1)S(1)} %pad_maximum_fusion.refs_0_), channel_id=1, source_target_pairs={{0,2},{1,3},{2,0},{3,1},{4,6},{5,7},{6,4},{7,5},{8,9},{9,8},{10,11... | collective-permute-start | bytes 983048 | tf_op jit(solution)/shard_map/ppermute | solution.py:456
  109.2 5.7 %collective-permute-start.29 = (bf16[512,128]{1,0:T(8,128)(2,1)S(1)}, bf16[512,128]{1,0:T(8,128)(2,1)S(1)}, u32[]{:S(2)}, u32[]{:S(2)}) collective-permute-start(bf16[512,128]{1,0:T(8,128)(2,1)S(1)} %get-tuple-element.145), channel_id=1, source_target_pairs={{0,248},{8,16},{16,8},{24,32},{32,24},{40,48},{48,40},{56,64},{64,... | collective-permute-start | bytes 393224 | tf_op jit(solution)/shard_map/ppermute | solution.py:426
  111.9 8.4 %collective-permute-start.30 = (bf16[512,128]{1,0:T(8,128)(2,1)S(1)}, bf16[512,128]{1,0:T(8,128)(2,1)S(1)}, u32[]{:S(2)}, u32[]{:S(2)}) collective-permute-start(bf16[512,128]{1,0:T(8,128)(2,1)S(1)} %get-tuple-element.146), channel_id=1, source_target_pairs={{0,240},{8,24},{16,0},{24,40},{32,16},{40,56},{48,32},{56,72},{64,... | collective-permute-start | bytes 393224 | tf_op jit(solution)/shard_map/ppermute | solution.py:426
  (35 other events, 439.9 us)
where the time goes:
time: 127 us
  starting transfers between devices  52.5 us (41%)
  waiting for transfers between devices  41.6 us (33%)
  Pallas kernels  26.4 us (21%)
  local copies, waits for them, and re-layouts  3.19 us (3%)
  other arithmetic  1.97 us (2%)
    ppermute x20, starting transfers between devices, along(): lax.ppermute(value, axis, [(i, target(i)) for i in range(lax.axis_size(ax...  38.2 us
    pallas_call x13, Pallas kernels, run(): pl.pallas_call(kernel, grid=(1,), out_shape=outs, in_specs=specs, out_spe...  26.3 us
    ppermute x20, waiting for transfers between devices, along(): lax.ppermute(value, axis, [(i, target(i)) for i in range(lax.axis_size(ax...  19.7 us
    ppermute x3, waiting for transfers between devices, z_flip(): return lax.ppermute(value, BOTH, pairs)  13.7 us
    ppermute x6, starting transfers between devices, outer_step(): return lax.ppermute(value, BOTH, pairs)  7.27 us
    ppermute x6, starting transfers between devices, inner_step(): return lax.ppermute(value, BOTH, pairs)  6.51 us
    ppermute x6, waiting for transfers between devices, inner_step(): return lax.ppermute(value, BOTH, pairs)  6.49 us
  transfers between devices with their start and end apart: 35, of which 17 were waited for; matrix products, arithmetic and copies ran while one was open for 2% of the time, Pallas kernels for 4%

commit v1 on v0

--- a/solution.py
+++ b/solution.py
@@ -124,10 +124,12 @@
             aug = jnp.where(row16 < 12, aug, jnp.where(row16 < 15, 1.0, 0.0))
             augq_ref[...] = aug.reshape(N, N).T.astype(BF)
 
-    for load in loads:
-        load.wait()
+    loads[0].wait()
+    loads[1].wait()
     k_ref[...] = dot(normed_ref[...], wk_ref[...]).astype(BF)
     v_ref[...] = dot(normed_ref[...], wv_ref[...]).astype(BF)
+    for load in loads[2:]:
+        load.wait()
     query = (dot(normed_ref[0:N, :], wq_ref[...]).astype(BF) * 0.125).astype(BF)
 
     row_n = lax.broadcasted_iota(jnp.int32, (N, N), 0)
@@ -164,6 +166,7 @@
         gp = d_heads[:, cols]
         q_parts = [qp * m for m in masks_b]
         g_parts = [gp * m for m in masks_b]
+        shares = []
         probs = []
         probs_b = []
         outs = []
@@ -174,10 +177,10 @@
             scores = dot(left, keys_aug, 1, 1)
             top = jnp.max(scores, axis=1, keepdims=True)
             weights = jnp.exp(scores - top)
-            prob = weights * (1.0 / jnp.sum(weights, axis=1, keepdims=True))
-            probs.append(prob)
-            probs_b.append(prob.astype(BF))
-            outs.append(dot(probs_b[t], values))
+            shares.append(1.0 / jnp.sum(weights, axis=1, keepdims=True))
+            probs.append(weights)
+            probs_b.append(weights.astype(BF))
+            outs.append(dot(probs_b[t], values) * shares[t])
         merged = jnp.where(first, outs[0], outs[1]).astype(BF)
         ho_ref[:, cols] = merged
         inner = gp.astype(F32) * merged.astype(F32)
@@ -188,8 +191,10 @@
             d_prob = dot(g_parts[t], values, 1, 1)
             d_score = (probs[t] * (d_prob - delta)).astype(BF)
             scores_b.append(d_score)
-            dqs.append(dot(d_score, keys))
+            dqs.append(dot(d_score, keys) * shares[t])
         dq_ref[:, cols] = (jnp.where(first, dqs[0], dqs[1]) * 0.125).astype(BF)
+        q_parts = [(q.astype(F32) * share).astype(BF) for q, share in zip(q_parts, shares)]
+        g_parts = [(g.astype(F32) * share).astype(BF) for g, share in zip(g_parts, shares)]
         dk_t_ref[cols, :] = dot(
             jnp.concatenate(q_parts, axis=0), jnp.concatenate(scores_b, axis=0), 0, 0
         ).astype(BF)

time: 127 us -> 126 us (level)
  no operation moved by 1% of the time
where the time goes in v1:
time: 126 us
  starting transfers between devices  52.6 us (42%)
  waiting for transfers between devices  41.5 us (33%)
  Pallas kernels  25.8 us (20%)
  local copies, waits for them, and re-layouts  3.19 us (3%)
  other arithmetic  1.97 us (2%)
    ppermute x20, starting transfers between devices, along(): lax.ppermute(value, axis, [(i, target(i)) for i in range(lax.axis_size(ax...  38.2 us
    pallas_call x13, Pallas kernels, run(): pl.pallas_call(kernel, grid=(1,), out_shape=outs, in_specs=specs, out_spe...  25.7 us
    ppermute x20, waiting for transfers between devices, along(): lax.ppermute(value, axis, [(i, target(i)) for i in range(lax.axis_size(ax...  19.7 us
    ppermute x3, waiting for transfers between devices, z_flip(): return lax.ppermute(value, BOTH, pairs)  13.7 us
    ppermute x6, starting transfers between devices, outer_step(): return lax.ppermute(value, BOTH, pairs)  7.25 us
    ppermute x6, starting transfers between devices, inner_step(): return lax.ppermute(value, BOTH, pairs)  6.51 us
    ppermute x6, waiting for transfers between devices, inner_step(): return lax.ppermute(value, BOTH, pairs)  6.46 us
  transfers between devices with their start and end apart: 35, of which 17 were waited for; matrix products, arithmetic and copies ran while one was open for 2% of the time, Pallas kernels for 4%

profile of v1, /device:TPU:1, one launch (start us, length us, event | category | flops | bytes accessed | tf_op | source)
XLA Modules:
  0.0 126.2 jit_solution(7147942602063870092)
XLA Ops:
  0.6 1.7 %shard_map.198 = (bf16[144,512]{1,0:T(8,128)(2,1)}, bf16[144,512]{1,0:T(8,128)(2,1)}) custom-call(bf16[128,512]{1,0:T(8,128)(2,1)} %refs_5_.1, bf16[3,128]{1,0:T(4,128)(2,1)} %pos_ref.1, bf16[8,128]{1,0:T(8,128)(2,1)} %bias_ref.1, bf16[128,512]{1,0:T(8,128)(2,1)} %refs_7_.1, s32[1,128]{1,0:T(1,128)} %bitcast.13), custom_call_target="tpu_custom_call" | custom-call | flops 1000000 | bytes 4000000 | tf_op jit(solution)/shard_map/pallas_call | solution.py:270
  2.4 4.3 %collective-permute-start.1 = (bf16[144,512]{1,0:T(8,128)(2,1)}, bf16[144,512]{1,0:T(8,128)(2,1)S(1)}, u32[]{:S(2)}, u32[]{:S(2)}) collective-permute-start(bf16[144,512]{1,0:T(8,128)(2,1)} %get-tuple-element.87), channel_id=1, source_target_pairs={{0,7},{1,2},{2,1},{3,4},{4,3},{5,6},{6,5},{7,0},{8,15},{9,10},{10,... | collective-permute-start | bytes 442376 | tf_op jit(solution)/shard_map/ppermute | solution.py:431
  6.7 8.8 %collective-permute-start.7 = (bf16[144,512]{1,0:T(8,128)(2,1)}, bf16[144,512]{1,0:T(8,128)(2,1)S(1)}, u32[]{:S(2)}, u32[]{:S(2)}) collective-permute-start(bf16[144,512]{1,0:T(8,128)(2,1)} %get-tuple-element.88.refs_0_), channel_id=1, source_target_pairs={{0,24},{8,240},{16,40},{24,0},{32,56},{40,16},{48,72},{56,32},{64,... | collective-permute-start | bytes 442376 | tf_op jit(solution)/shard_map/ppermute | solution.py:431
  16.7 5.1 %collective-permute-start.3 = (bf16[144,512]{1,0:T(8,128)(2,1)}, bf16[144,512]{1,0:T(8,128)(2,1)S(1)}, u32[]{:S(2)}, u32[]{:S(2)}) collective-permute-start(bf16[144,512]{1,0:T(8,128)(2,1)} %get-tuple-element.88.refs_0_), channel_id=1, source_target_pairs={{0,16},{8,248},{16,32},{24,8},{32,48},{40,24},{48,64},{56,40},{64,... | collective-permute-start | bytes 442376 | tf_op jit(solution)/shard_map/ppermute | solution.py:431
  21.8 1.9 %collective-permute-start.5 = (bf16[144,512]{1,0:T(8,128)(2,1)}, bf16[144,512]{1,0:T(8,128)(2,1)S(1)}, u32[]{:S(2)}, u32[]{:S(2)}) collective-permute-start(bf16[144,512]{1,0:T(8,128)(2,1)} %get-tuple-element.88.refs_0_), channel_id=1, source_target_pairs={{0,8},{8,0},{16,24},{24,16},{32,40},{40,32},{48,56},{56,48},{64,72... | collective-permute-start | bytes 442376 | tf_op jit(solution)/shard_map/ppermute | solution.py:431
  25.8 2.7 %collective-permute-done.2.refs_1_ = bf16[144,512]{1,0:T(8,128)(2,1)S(1)} collective-permute-done((bf16[144,512]{1,0:T(8,128)(2,1)}, bf16[144,512]{1,0:T(8,128)(2,1)S(1)}, u32[]{:S(2)}, u32[]{:S(2)}) %collective-permute-start.2) | collective-permute-done | bytes 147488 | tf_op jit(solution)/shard_map/ppermute | solution.py:431
  29.1 15.6 %shard_map.199 = (bf16[16,80,512]{2,1,0:T(8,128)(2,1)}, bf16[16,80,512]{2,1,0:T(8,128)(2,1)}, bf16[128,512]{1,0:T(8,128)(2,1)}, bf16[128,512]{1,0:T(8,128)(2,1)}...) custom-call(s32[7]{0:T(128)} %get-tuple-element.166.offs_ref, ...), custom_call_target="tpu_custom_call" | custom-call | flops 6000000000 | bytes 4000000 | tf_op jit(solution)/shard_map/pallas_call | solution.py:270
  44.7 4.0 %collective-permute-start.8 = (bf16[16,80,512]{2,1,0:T(8,128)(2,1)}, bf16[16,80,512]{2,1,0:T(8,128)(2,1)S(1)}, u32[]{:S(2)}, u32[]{:S(2)}) collective-permute-start(bf16[16,80,512]{2,1,0:T(8,128)(2,1)} %get-tuple-element.92), channel_id=1, source_target_pairs={{0,8},{8,0},{16,24},{24,16},{32,40},{40,32},{48,56},{56,48},{64,72... | collective-permute-start | bytes 3932168 | tf_op jit(solution)/shard_map/ppermute | solution.py:431
  53.3 1.7 %collective-permute-start.10 = (bf16[4,80,512]{2,1,0:T(8,128)(2,1)S(1)}, bf16[4,80,512]{2,1,0:T(8,128)(2,1)S(1)}, u32[]{:S(2)}, u32[]{:S(2)}) collective-permute-start(bf16[4,80,512]{2,1,0:T(8,128)(2,1)S(1)} %get-tuple-element.101), channel_id=1, source_target_pairs={{0,2},{1,3},{2,0},{3,1},{4,6},{5,7},{6,4},{7,5},{8,9},{9,8},{10,11... | collective-permute-start | bytes 983048 | tf_op jit(solution)/shard_map/ppermute | solution.py:461
  56.5 6.1 %collective-permute-done.13.refs_3_ = bf16[512,128]{1,0:T(8,128)(2,1)S(1)} collective-permute-done((bf16[512,128]{1,0:T(8,128)(2,1)S(1)}, bf16[512,128]{1,0:T(8,128)(2,1)S(1)}, u32[]{:S(2)}, u32[]{:S(2)}) %collective-permute-start.13) | collective-permute-done | bytes 131104 | tf_op jit(solution)/shard_map/ppermute | solution.py:431
  73.9 3.3 %collective-permute-done.19.b_ref = bf16[80,512]{1,0:T(8,128)(2,1)S(1)} collective-permute-done((bf16[80,512]{1,0:T(8,128)(2,1)S(1)}, bf16[80,512]{1,0:T(8,128)(2,1)S(1)}, u32[]{:S(2)}, u32[]{:S(2)}) %collective-permute-start.19) | collective-permute-done | bytes 81952 | tf_op jit(solution)/shard_map/ppermute | solution.py:471
  77.4 1.6 %shard_map.205 = bf16[128,512]{1,0:T(8,128)(2,1)} custom-call(s32[2]{0:T(128)S(1)} %copy-done.10, s32[1,128]{1,0:T(1,128)S(1)} %bitcast.14, bf16[128,512]{1,0:T(8,128)(2,1)S(1)} %collective-permute-done.17.one_ref, bf16[128,512]{1,0:T(8,128)(2,1)S(1)} %collective-permute-done.18.two_ref, bf16[128,512]{1,0:T(8,128)(2,1)S(1)} %copy-done.7, ...), custom_call_target="tpu_custom_call" | custom-call | flops 1000000 | bytes 4000000 | tf_op jit(solution)/shard_map/pallas_call | solution.py:270
  79.0 3.1 %collective-permute-done.20.b_ref = bf16[80,512]{1,0:T(8,128)(2,1)S(1)} collective-permute-done((bf16[80,512]{1,0:T(8,128)(2,1)S(1)}, bf16[80,512]{1,0:T(8,128)(2,1)S(1)}, u32[]{:S(2)}, u32[]{:S(2)}) %collective-permute-start.20) | collective-permute-done | bytes 81952 | tf_op jit(solution)/shard_map/ppermute | solution.py:471
  82.5 7.3 %collective-permute-done.21.b_ref = bf16[80,512]{1,0:T(8,128)(2,1)S(1)} collective-permute-done((bf16[80,512]{1,0:T(8,128)(2,1)S(1)}, bf16[80,512]{1,0:T(8,128)(2,1)S(1)}, u32[]{:S(2)}, u32[]{:S(2)}) %collective-permute-start.21) | collective-permute-done | bytes 81952 | tf_op jit(solution)/shard_map/ppermute | solution.py:471
  89.9 7.6 %collective-permute-start.22 = (bf16[80,512]{1,0:T(8,128)(2,1)S(1)}, bf16[80,512]{1,0:T(8,128)(2,1)S(1)}, u32[]{:S(2)}, u32[]{:S(2)}) collective-permute-start(bf16[80,512]{1,0:T(8,128)(2,1)S(1)} %shard_map.208), channel_id=1, source_target_pairs={{0,8},{8,0},{16,24},{24,16},{32,40},{40,32},{48,56},{56,48},{64,72... | collective-permute-start | bytes 245768 | tf_op jit(solution)/shard_map/ppermute | solution.py:431
  98.4 1.6 %collective-permute-start.25 = (bf16[80,512]{1,0:T(8,128)(2,1)S(1)}, bf16[80,512]{1,0:T(8,128)(2,1)S(1)}, u32[]{:S(2)}, u32[]{:S(2)}) collective-permute-start(bf16[80,512]{1,0:T(8,128)(2,1)S(1)} %shard_map.208), channel_id=1, source_target_pairs={{0,129},{1,128},{2,131},{3,130},{4,133},{5,132},{6,135},{7,134},{8... | collective-permute-start | bytes 245768 | tf_op jit(solution)/shard_map/ppermute | solution.py:467
  101.7 1.5 %collective-permute-done.25 = bf16[80,512]{1,0:T(8,128)(2,1)S(1)} collective-permute-done((bf16[80,512]{1,0:T(8,128)(2,1)S(1)}, bf16[80,512]{1,0:T(8,128)(2,1)S(1)}, u32[]{:S(2)}, u32[]{:S(2)}) %collective-permute-start.25) | collective-permute-done | bytes 81952 | tf_op jit(solution)/shard_map/ppermute | solution.py:467
  103.2 1.6 %collective-permute-done.24 = bf16[80,512]{1,0:T(8,128)(2,1)S(1)} collective-permute-done((bf16[80,512]{1,0:T(8,128)(2,1)S(1)}, bf16[80,512]{1,0:T(8,128)(2,1)S(1)}, u32[]{:S(2)}, u32[]{:S(2)}) %collective-permute-start.24) | collective-permute-done | bytes 81952 | tf_op jit(solution)/shard_map/ppermute | solution.py:467
  104.8 3.0 %collective-permute-start.28 = (bf16[4,80,512]{2,1,0:T(8,128)(2,1)S(1)}, bf16[4,80,512]{2,1,0:T(8,128)(2,1)S(1)}, u32[]{:S(2)}, u32[]{:S(2)}) collective-permute-start(bf16[4,80,512]{2,1,0:T(8,128)(2,1)S(1)} %pad_maximum_fusion.refs_0_), channel_id=1, source_target_pairs={{0,6},{1,7},{2,4},{3,5},{4,2},{5,3},{6,0},{7,1},{8,137},{9,136},{1... | collective-permute-start | bytes 983048 | tf_op jit(solution)/shard_map/ppermute | solution.py:461
  108.6 2.8 %collective-permute-start.29 = (bf16[512,128]{1,0:T(8,128)(2,1)S(1)}, bf16[512,128]{1,0:T(8,128)(2,1)S(1)}, u32[]{:S(2)}, u32[]{:S(2)}) collective-permute-start(bf16[512,128]{1,0:T(8,128)(2,1)S(1)} %get-tuple-element.145), channel_id=1, source_target_pairs={{0,248},{8,16},{16,8},{24,32},{32,24},{40,48},{48,40},{56,64},{64,... | collective-permute-start | bytes 393224 | tf_op jit(solution)/shard_map/ppermute | solution.py:431
  111.4 2.9 %collective-permute-done.29.refs_1_ = bf16[512,128]{1,0:T(8,128)(2,1)S(1)} collective-permute-done((bf16[512,128]{1,0:T(8,128)(2,1)S(1)}, bf16[512,128]{1,0:T(8,128)(2,1)S(1)}, u32[]{:S(2)}, u32[]{:S(2)}) %collective-permute-start.29) | collective-permute-done | bytes 131104 | tf_op jit(solution)/shard_map/ppermute | solution.py:431
  114.3 5.4 %collective-permute-done.30.refs_2_ = bf16[512,128]{1,0:T(8,128)(2,1)S(1)} collective-permute-done((bf16[512,128]{1,0:T(8,128)(2,1)S(1)}, bf16[512,128]{1,0:T(8,128)(2,1)S(1)}, u32[]{:S(2)}, u32[]{:S(2)}) %collective-permute-start.30) | collective-permute-done | bytes 131104 | tf_op jit(solution)/shard_map/ppermute | solution.py:431
  121.8 2.1 %shard_map.210 = (f32[512,512]{1,0:T(8,128)}, f32[512,512]{1,0:T(8,128)}, f32[512,512]{1,0:T(8,128)}, f32[512,512]{1,0:T(8,128)}, f32[512,512]{1,0:T(8,128)}) custom-call(s32[3]{0:T(128)S(1)} %pad_add_fusion.place_ref, bf16[4,80,512]{2,1,0:T(8,128)(2,1)S(1)} %pad_maximum_fusion.refs_0_, bf16[4,80,512]{2,1,0:T(8,128)(2,1)S(1)} %collective-permute-done.26.refs_1_, ...), custom_call_target="tpu_custom_call" | custom-call | flops 1000000 | bytes 4000000 | tf_op jit(solution)/shard_map/pallas_call | solution.py:270
  124.0 2.1 %shard_map.211 = (f32[512,512]{1,0:T(8,128)}, f32[512,512]{1,0:T(8,128)}, f32[512,512]{1,0:T(8,128)}, f32[512,512]{1,0:T(8,128)}, f32[512,512]{1,0:T(8,128)}) custom-call(s32[3]{0:T(128)S(1)} %pad_add_fusion.place_ref, ...), custom_call_target="tpu_custom_call", output_to_operand_aliasing={{0}: (5, {}), {1}: (6, {}), {2}: (7, {}), {3}: (8, {}), {4}... | custom-call | flops 1000000 | bytes 4000000 | tf_op jit(solution)/shard_map/pallas_call | solution.py:270
  (114 shorter events, 27.3 us)
Async XLA Ops:
  2.4 14.3 %collective-permute-start.1 = (bf16[144,512]{1,0:T(8,128)(2,1)}, bf16[144,512]{1,0:T(8,128)(2,1)S(1)}, u32[]{:S(2)}, u32[]{:S(2)}) collective-permute-start(bf16[144,512]{1,0:T(8,128)(2,1)} %get-tuple-element.87), channel_id=1, source_target_pairs={{0,7},{1,2},{2,1},{3,4},{4,3},{5,6},{6,5},{7,0},{8,15},{9,10},{10,... | collective-permute-start | bytes 442376 | tf_op jit(solution)/shard_map/ppermute | solution.py:431
  6.7 15.1 %collective-permute-start = (bf16[144,512]{1,0:T(8,128)(2,1)}, bf16[144,512]{1,0:T(8,128)(2,1)S(1)}, u32[]{:S(2)}, u32[]{:S(2)}) collective-permute-start(bf16[144,512]{1,0:T(8,128)(2,1)} %get-tuple-element.87), channel_id=1, source_target_pairs={{0,1},{1,0},{2,3},{3,2},{4,5},{5,4},{6,7},{7,6},{8,9},{9,8},{10,11... | collective-permute-start | bytes 442376 | tf_op jit(solution)/shard_map/ppermute | solution.py:431
  6.7 17.0 %collective-permute-start.7 = (bf16[144,512]{1,0:T(8,128)(2,1)}, bf16[144,512]{1,0:T(8,128)(2,1)S(1)}, u32[]{:S(2)}, u32[]{:S(2)}) collective-permute-start(bf16[144,512]{1,0:T(8,128)(2,1)} %get-tuple-element.88.refs_0_), channel_id=1, source_target_pairs={{0,24},{8,240},{16,40},{24,0},{32,56},{40,16},{48,72},{56,32},{64,... | collective-permute-start | bytes 442376 | tf_op jit(solution)/shard_map/ppermute | solution.py:431
  15.4 10.0 %collective-permute-start.6 = (bf16[144,512]{1,0:T(8,128)(2,1)}, bf16[144,512]{1,0:T(8,128)(2,1)S(1)}, u32[]{:S(2)}, u32[]{:S(2)}) collective-permute-start(bf16[144,512]{1,0:T(8,128)(2,1)} %get-tuple-element.88.refs_0_), channel_id=1, source_target_pairs={{0,240},{8,24},{16,0},{24,40},{32,16},{40,56},{48,32},{56,72},{64,... | collective-permute-start | bytes 442376 | tf_op jit(solution)/shard_map/ppermute | solution.py:431
  15.5 10.0 %collective-permute-start.4 = (bf16[144,512]{1,0:T(8,128)(2,1)}, bf16[144,512]{1,0:T(8,128)(2,1)S(1)}, u32[]{:S(2)}, u32[]{:S(2)}) collective-permute-start(bf16[144,512]{1,0:T(8,128)(2,1)} %get-tuple-element.88.refs_0_), channel_id=1, source_target_pairs={{0,232},{8,32},{16,248},{24,48},{32,8},{40,64},{48,24},{56,80},{64... | collective-permute-start | bytes 442376 | tf_op jit(solution)/shard_map/ppermute | solution.py:431
  16.7 9.1 %collective-permute-start.3 = (bf16[144,512]{1,0:T(8,128)(2,1)}, bf16[144,512]{1,0:T(8,128)(2,1)S(1)}, u32[]{:S(2)}, u32[]{:S(2)}) collective-permute-start(bf16[144,512]{1,0:T(8,128)(2,1)} %get-tuple-element.88.refs_0_), channel_id=1, source_target_pairs={{0,16},{8,248},{16,32},{24,8},{32,48},{40,24},{48,64},{56,40},{64,... | collective-permute-start | bytes 442376 | tf_op jit(solution)/shard_map/ppermute | solution.py:431
  44.7 6.9 %collective-permute-start.8 = (bf16[16,80,512]{2,1,0:T(8,128)(2,1)}, bf16[16,80,512]{2,1,0:T(8,128)(2,1)S(1)}, u32[]{:S(2)}, u32[]{:S(2)}) collective-permute-start(bf16[16,80,512]{2,1,0:T(8,128)(2,1)} %get-tuple-element.92), channel_id=1, source_target_pairs={{0,8},{8,0},{16,24},{24,16},{32,40},{40,32},{48,56},{56,48},{64,72... | collective-permute-start | bytes 3932168 | tf_op jit(solution)/shard_map/ppermute | solution.py:431
  52.5 11.7 %collective-permute-start.12 = (bf16[3,512,128]{2,1,0:T(8,128)(2,1)S(1)}, bf16[3,512,128]{2,1,0:T(8,128)(2,1)S(1)}, u32[]{:S(2)}, u32[]{:S(2)}) collective-permute-start(bf16[3,512,128]{2,1,0:T(8,128)(2,1)S(1)} %copy-done.12), channel_id=1, source_target_pairs={{0,8},{8,0},{16,24},{24,16},{32,40},{40,32},{48,56},{56,48},{64,72... | collective-permute-start | bytes 1179656 | tf_op jit(solution)/shard_map/ppermute | solution.py:431
  52.9 9.6 %collective-permute-start.9 = (bf16[4,80,512]{2,1,0:T(8,128)(2,1)S(1)}, bf16[4,80,512]{2,1,0:T(8,128)(2,1)S(1)}, u32[]{:S(2)}, u32[]{:S(2)}) collective-permute-start(bf16[4,80,512]{2,1,0:T(8,128)(2,1)S(1)} %get-tuple-element.100), channel_id=1, source_target_pairs={{0,4},{1,5},{2,6},{3,7},{4,0},{5,1},{6,2},{7,3},{8,136},{9,137},{1... | collective-permute-start | bytes 983048 | tf_op jit(solution)/shard_map/ppermute | solution.py:461
  53.3 10.0 %collective-permute-start.10 = (bf16[4,80,512]{2,1,0:T(8,128)(2,1)S(1)}, bf16[4,80,512]{2,1,0:T(8,128)(2,1)S(1)}, u32[]{:S(2)}, u32[]{:S(2)}) collective-permute-start(bf16[4,80,512]{2,1,0:T(8,128)(2,1)S(1)} %get-tuple-element.101), channel_id=1, source_target_pairs={{0,2},{1,3},{2,0},{3,1},{4,6},{5,7},{6,4},{7,5},{8,9},{9,8},{10,11... | collective-permute-start | bytes 983048 | tf_op jit(solution)/shard_map/ppermute | solution.py:461
  55.0 9.2 %collective-permute-start.11 = (bf16[4,80,512]{2,1,0:T(8,128)(2,1)S(1)}, bf16[4,80,512]{2,1,0:T(8,128)(2,1)S(1)}, u32[]{:S(2)}, u32[]{:S(2)}) collective-permute-start(bf16[4,80,512]{2,1,0:T(8,128)(2,1)S(1)} %get-tuple-element.102), channel_id=1, source_target_pairs={{0,6},{1,7},{2,4},{3,5},{4,2},{5,3},{6,0},{7,1},{8,137},{9,136},{1... | collective-permute-start | bytes 983048 | tf_op jit(solution)/shard_map/ppermute | solution.py:461
  56.5 6.1 %collective-permute-start.13 = (bf16[512,128]{1,0:T(8,128)(2,1)S(1)}, bf16[512,128]{1,0:T(8,128)(2,1)S(1)}, u32[]{:S(2)}, u32[]{:S(2)}) collective-permute-start(bf16[512,128]{1,0:T(8,128)(2,1)S(1)} %copy-done.23), channel_id=1, source_target_pairs={{0,232},{8,32},{16,248},{24,48},{32,8},{40,64},{48,24},{56,80},{64... | collective-permute-start | bytes 393224 | tf_op jit(solution)/shard_map/ppermute | solution.py:431
  64.9 8.8 %collective-permute-start.17 = (bf16[128,512]{1,0:T(8,128)(2,1)S(1)}, bf16[128,512]{1,0:T(8,128)(2,1)S(1)}, u32[]{:S(2)}, u32[]{:S(2)}) collective-permute-start(bf16[128,512]{1,0:T(8,128)(2,1)S(1)} %copy-done.22), channel_id=1, source_target_pairs={{0,1},{1,0},{2,3},{3,2},{4,5},{5,4},{6,7},{7,6},{8,9},{9,8},{10,11... | collective-permute-start | bytes 393224 | tf_op jit(solution)/shard_map/ppermute | solution.py:431
  66.1 7.6 %collective-permute-start.18 = (bf16[128,512]{1,0:T(8,128)(2,1)S(1)}, bf16[128,512]{1,0:T(8,128)(2,1)S(1)}, u32[]{:S(2)}, u32[]{:S(2)}) collective-permute-start(bf16[128,512]{1,0:T(8,128)(2,1)S(1)} %copy-done.21), channel_id=1, source_target_pairs={{0,7},{1,2},{2,1},{3,4},{4,3},{5,6},{6,5},{7,0},{8,15},{9,10},{10,... | collective-permute-start | bytes 393224 | tf_op jit(solution)/shard_map/ppermute | solution.py:431
  68.9 4.8 %collective-permute-start.16 = (bf16[80,512]{1,0:T(8,128)(2,1)S(1)}, bf16[80,512]{1,0:T(8,128)(2,1)S(1)}, u32[]{:S(2)}, u32[]{:S(2)}) collective-permute-start(bf16[80,512]{1,0:T(8,128)(2,1)S(1)} %get-tuple-element.117), channel_id=1, source_target_pairs={{0,129},{1,128},{2,131},{3,130},{4,133},{5,132},{6,135},{7,134},{8... | collective-permute-start | bytes 245768 | tf_op jit(solution)/shard_map/ppermute | solution.py:467
  77.2 4.9 %collective-permute-start.20 = (bf16[80,512]{1,0:T(8,128)(2,1)S(1)}, bf16[80,512]{1,0:T(8,128)(2,1)S(1)}, u32[]{:S(2)}, u32[]{:S(2)}) collective-permute-start(bf16[80,512]{1,0:T(8,128)(2,1)S(1)} %shard_map.204.a_ref), channel_id=1, source_target_pairs={{0,32},{1,33},{2,34},{3,35},{4,36},{5,37},{6,38},{7,39},{8,40},{9,... | collective-permute-start | bytes 245768 | tf_op jit(solution)/shard_map/ppermute | solution.py:471
  82.1 7.7 %collective-permute-start.21 = (bf16[80,512]{1,0:T(8,128)(2,1)S(1)}, bf16[80,512]{1,0:T(8,128)(2,1)S(1)}, u32[]{:S(2)}, u32[]{:S(2)}) collective-permute-start(bf16[80,512]{1,0:T(8,128)(2,1)S(1)} %shard_map.206.a_ref), channel_id=1, source_target_pairs={{0,64},{1,65},{2,66},{3,67},{4,68},{5,69},{6,70},{7,71},{8,72},{9,... | collective-permute-start | bytes 245768 | tf_op jit(solution)/shard_map/ppermute | solution.py:471
  89.9 8.6 %collective-permute-start.22 = (bf16[80,512]{1,0:T(8,128)(2,1)S(1)}, bf16[80,512]{1,0:T(8,128)(2,1)S(1)}, u32[]{:S(2)}, u32[]{:S(2)}) collective-permute-start(bf16[80,512]{1,0:T(8,128)(2,1)S(1)} %shard_map.208), channel_id=1, source_target_pairs={{0,8},{8,0},{16,24},{24,16},{32,40},{40,32},{48,56},{56,48},{64,72... | collective-permute-start | bytes 245768 | tf_op jit(solution)/shard_map/ppermute | solution.py:431
  98.4 4.8 %collective-permute-start.25 = (bf16[80,512]{1,0:T(8,128)(2,1)S(1)}, bf16[80,512]{1,0:T(8,128)(2,1)S(1)}, u32[]{:S(2)}, u32[]{:S(2)}) collective-permute-start(bf16[80,512]{1,0:T(8,128)(2,1)S(1)} %shard_map.208), channel_id=1, source_target_pairs={{0,129},{1,128},{2,131},{3,130},{4,133},{5,132},{6,135},{7,134},{8... | collective-permute-start | bytes 245768 | tf_op jit(solution)/shard_map/ppermute | solution.py:467
  104.8 15.8 %collective-permute-start.28 = (bf16[4,80,512]{2,1,0:T(8,128)(2,1)S(1)}, bf16[4,80,512]{2,1,0:T(8,128)(2,1)S(1)}, u32[]{:S(2)}, u32[]{:S(2)}) collective-permute-start(bf16[4,80,512]{2,1,0:T(8,128)(2,1)S(1)} %pad_maximum_fusion.refs_0_), channel_id=1, source_target_pairs={{0,6},{1,7},{2,4},{3,5},{4,2},{5,3},{6,0},{7,1},{8,137},{9,136},{1... | collective-permute-start | bytes 983048 | tf_op jit(solution)/shard_map/ppermute | solution.py:461
  107.9 12.8 %collective-permute-start.27 = (bf16[4,80,512]{2,1,0:T(8,128)(2,1)S(1)}, bf16[4,80,512]{2,1,0:T(8,128)(2,1)S(1)}, u32[]{:S(2)}, u32[]{:S(2)}) collective-permute-start(bf16[4,80,512]{2,1,0:T(8,128)(2,1)S(1)} %pad_maximum_fusion.refs_0_), channel_id=1, source_target_pairs={{0,4},{1,5},{2,6},{3,7},{4,0},{5,1},{6,2},{7,3},{8,136},{9,137},{1... | collective-permute-start | bytes 983048 | tf_op jit(solution)/shard_map/ppermute | solution.py:461
  107.9 12.8 %collective-permute-start.26 = (bf16[4,80,512]{2,1,0:T(8,128)(2,1)S(1)}, bf16[4,80,512]{2,1,0:T(8,128)(2,1)S(1)}, u32[]{:S(2)}, u32[]{:S(2)}) collective-permute-start(bf16[4,80,512]{2,1,0:T(8,128)(2,1)S(1)} %pad_maximum_fusion.refs_0_), channel_id=1, source_target_pairs={{0,2},{1,3},{2,0},{3,1},{4,6},{5,7},{6,4},{7,5},{8,9},{9,8},{10,11... | collective-permute-start | bytes 983048 | tf_op jit(solution)/shard_map/ppermute | solution.py:461
  108.6 5.8 %collective-permute-start.29 = (bf16[512,128]{1,0:T(8,128)(2,1)S(1)}, bf16[512,128]{1,0:T(8,128)(2,1)S(1)}, u32[]{:S(2)}, u32[]{:S(2)}) collective-permute-start(bf16[512,128]{1,0:T(8,128)(2,1)S(1)} %get-tuple-element.145), channel_id=1, source_target_pairs={{0,248},{8,16},{16,8},{24,32},{32,24},{40,48},{48,40},{56,64},{64,... | collective-permute-start | bytes 393224 | tf_op jit(solution)/shard_map/ppermute | solution.py:431
  111.4 8.4 %collective-permute-start.30 = (bf16[512,128]{1,0:T(8,128)(2,1)S(1)}, bf16[512,128]{1,0:T(8,128)(2,1)S(1)}, u32[]{:S(2)}, u32[]{:S(2)}) collective-permute-start(bf16[512,128]{1,0:T(8,128)(2,1)S(1)} %get-tuple-element.146), channel_id=1, source_target_pairs={{0,240},{8,24},{16,0},{24,40},{32,16},{40,56},{48,32},{56,72},{64,... | collective-permute-start | bytes 393224 | tf_op jit(solution)/shard_map/ppermute | solution.py:431
  (35 other events, 439.9 us)
